TPU v7x, 32 devices: a whole 2x2x4 slice. The times are simulated.
32 devices in a mesh: sx: 4 (over x, core), sy: 8 (over z, y).
Axes of the slice: x: 2, y: 2, z: 4, core: 2. Of those that a mesh axis runs over, the one named last changes fastest.
Arguments:
- loadings: bfloat16 [64, 16, 1024], P(None, 'sx', 'sy'), may hold values from 0.099609375 to 1
- gene_factors: bfloat16 [96, 64, 128], P('sy'), may hold values from 0.019897461 to 0.19921875
- counts: bfloat16 [4, 8, 32, 128, 512], P('sx', 'sy'), may hold values from 0 to 6
- block_ids: int32 [4, 8, 32], P('sx', 'sy'), may hold values from 0 to 95, as said below
- live: int32 [4, 8], P('sx', 'sy'), may hold values from 1 to 32, as said below
Outputs:
- grad_loadings: float32 [64, 16, 1024], P(None, 'sx', 'sy')
- grad_genes: float32 [96, 64, 128], P('sy')
Inputs may be any that keep to these rules, and one draw needn't show every extreme that they name: `block_ids`: the 32 entries of one tile are different gene blocks; slots from live onward are ignored. `live`: some tile uses all 32 slots.
All inputs are finite; a program needn't handle non-finite values.
Results may differ from a plain program's by a relative error of at most 0.0003.
Values may be sent and summed in bfloat16 or wider, within the bound.
A program may use at most 64 MiB of HBM per device.

v0:
```python
import jax
import jax.numpy as jnp
from jax import lax
from jax.sharding import PartitionSpec as P


def extended(value, sides, width):
    for axis, dim in sides:
        devices, length = (lax.axis_size(axis), value.shape[dim])
        up = [(i, (i + 1) % devices) for i in range(devices - 1)]
        down = [(j, i) for i, j in up]
        last = lax.slice_in_dim(value, length - width, length, axis=dim)
        initial = lax.slice_in_dim(value, 0, width, axis=dim)
        before = lax.ppermute(last, axis, up)
        after = lax.ppermute(initial, axis, down)
        value = jnp.concatenate([before, value, after], axis=dim)
    return value


def on_device(loadings, gene_factors, counts, block_ids, live):
    nfac = loadings.shape[0]
    rows = loadings.shape[1]
    cols = loadings.shape[2]
    spots = rows * cols
    factors = lax.all_gather(gene_factors, "sy", axis=0, tiled=True)
    wflat = loadings.reshape(nfac, spots)
    tile_counts = counts[0, 0]
    tile_ids = block_ids[0, 0]

    def step(n, carry):
        grad_part, dense_acc = carry
        block = tile_ids[n]
        block_factor = lax.dynamic_index_in_dim(factors, block, 0, keepdims=False)
        block_counts = lax.dynamic_index_in_dim(tile_counts, n, 0, keepdims=False)
        rate = lax.dot_general(
            block_factor, wflat, (((0,), (0,)), ((), ())), preferred_element_type=jnp.float32
        )
        ratio = (1.0 - block_counts.astype(jnp.float32) / rate).astype(jnp.bfloat16)
        grad_part = grad_part + lax.dot_general(
            block_factor, ratio, (((1,), (0,)), ((), ())), preferred_element_type=jnp.float32
        )
        gene_term = lax.dot_general(
            wflat, ratio, (((1,), (1,)), ((), ())), preferred_element_type=jnp.float32
        )
        old = lax.dynamic_index_in_dim(dense_acc, block, 0, keepdims=True)
        dense_acc = lax.dynamic_update_index_in_dim(dense_acc, old + gene_term[None], block, 0)
        return (grad_part, dense_acc)

    start = jnp.zeros((nfac, spots), jnp.float32)
    dense = jnp.zeros(factors.shape, jnp.float32)
    grad_part, dense = lax.fori_loop(0, live[0, 0], step, (start, dense))
    padded = extended(loadings, (("sx", 1), ("sy", 2)), 1).astype(jnp.float32)
    beside = padded[:, 2:, 1:-1] + padded[:, :-2, 1:-1] + padded[:, 1:-1, 2:] + padded[:, 1:-1, :-2]
    laplace = 4.0 * loadings.astype(jnp.float32) - beside
    grad_loadings = grad_part.reshape(nfac, rows, cols) + 0.5 * laplace
    row_count = lax.axis_size("sx")
    slab = lax.psum_scatter(dense, "sy", scatter_dimension=0, tiled=True)
    summed = lax.psum(slab, "sx")
    grad_genes = summed / (spots * row_count)
    return (grad_loadings, grad_genes)


def solution(mesh):
    return jax.shard_map(
        on_device,
        mesh=mesh,
        in_specs=(
            P(None, "sx", "sy"),
            P("sy", None, None),
            P("sx", "sy", None, None, None),
            P("sx", "sy", None),
            P("sx", "sy"),
        ),
        out_specs=(P(None, "sx", "sy"), P("sy", None, None)),
        check_vma=False,
    )
```

profile of v0, /device:TPU:0, one launch (start us, length us, event | category | flops | bytes accessed | tf_op | source)
XLA Modules:
  0.0 351.4 jit_solution(15973220760348036679)
XLA Ops:
  7.2 0.7 all-gather.2.cloned.1.call-update
  8.0 0.9 copy.9
  8.8 48.3 %all-gather.2.cloned.1.call-done = bf16[96,64,128]{2,1,0:T(8,128)(2,1)} async-done(((bf16[12,64,128]{2,1,0:T(8,128)(2,1)}), bf16[96,64,128]{2,1,0:T(8,128)(2,1)}) %all-gather.2.cloned.1.call-update) | async-done | bytes 1572880 | tf_op jit(solution)/shard_map/all_gather | solution.py:25
  57.5 60.2 %while.12 = (s32[]{:T(128)}, f32[64,512]{1,0:T(8,128)S(1)}, f32[96,64,128]{2,1,0:T(8,128)S(1)}, s32[]{:T(128)}, s32[32]{0:T(128)S(1)}, /*index=5*/bf16[96,64,128...) while((s32[]{:T(128)}, f32[64,512]{1,0:T(8,128)S(1)}, ...), condition=%wide.region_1.2_spmd, body=%wide.region_0.1_spmd.sunk | while | flops 25468936 | bytes 1016029 | solution.py:51
  58.2 0.6 dynamic_slice.34
  60.7 1.1 fusion.33
  61.9 0.9 convolution_add_fusion.2
  63.6 0.6 dynamic_slice.34
  66.1 1.1 fusion.33
  67.3 0.9 convolution_add_fusion.2
  69.0 0.6 dynamic_slice.34
  71.5 1.1 fusion.33
  72.7 0.9 convolution_add_fusion.2
  74.4 0.6 dynamic_slice.34
  77.0 1.1 fusion.33
  78.1 0.9 convolution_add_fusion.2
  79.8 0.6 dynamic_slice.34
  82.4 1.1 fusion.33
  83.5 0.9 convolution_add_fusion.2
  85.3 0.6 dynamic_slice.34
  87.8 1.1 fusion.33
  88.9 0.9 convolution_add_fusion.2
  90.7 0.6 dynamic_slice.34
  93.2 1.1 fusion.33
  94.4 0.9 convolution_add_fusion.2
  96.1 0.6 dynamic_slice.34
  98.6 1.1 fusion.33
  99.8 0.9 convolution_add_fusion.2
  101.5 0.6 dynamic_slice.34
  104.0 1.1 fusion.33
  105.2 0.9 convolution_add_fusion.2
  106.9 0.6 dynamic_slice.34
  109.4 1.1 fusion.33
  110.6 0.9 convolution_add_fusion.2
  114.9 1.1 fusion.33
  116.0 0.9 convolution_add_fusion.2
  117.8 1.6 copy-done
  119.5 1.3 collective-permute-start.1
  120.8 34.2 %collective-permute-start = (bf16[64,1,128]{2,1,0:T(2,128)(2,1)S(1)}, bf16[64,1,128]{2,1,0:T(2,128)(2,1)S(1)}, u32[]{:S(2)}, u32[]{:S(2)}) collective-permute-start(bf16[64,1,128]{2,1,0:T(2,128)(2,1)S(1)} %get-tuple-element.66), channel_id=1, source_target_pairs={{0,8},{8,16},{16,24},{1,9},{9,17},{17,25},{2,10},{10,18},{18,26},{... | collective-permute-start | bytes 49160 | tf_op jit(solution)/shard_map/ppermute | solution.py:14
  155.1 0.8 collective-permute-done
  156.1 1.3 collective-permute-start.3
  157.4 62.7 %collective-permute-start.2 = (bf16[64,6,1]{2,1,0:T(8,128)(2,1)S(1)}, bf16[64,6,1]{2,1,0:T(8,128)(2,1)S(1)}, u32[]{:S(2)}, u32[]{:S(2)}) collective-permute-start(bf16[64,6,1]{2,1,0:T(8,128)(2,1)S(1)} %get-tuple-element.64), channel_id=1, source_target_pairs={{0,1},{1,2},{2,3},{3,4},{4,5},{5,6},{6,7},{8,9},{9,10},{10,11},{11... | collective-permute-start | bytes 2312 | tf_op jit(solution)/shard_map/ppermute | solution.py:14
  220.1 1.2 collective-permute-done.3
  221.3 2.5 collective-permute-done.2
  224.3 84.7 %reduce-scatter.2.cloned.1.call-done = f32[12,64,128]{2,1,0:T(8,128)} async-done(((f32[96,64,128]{2,1,0:T(8,128)}), f32[12,64,128]{2,1,0:T(8,128)}) %reduce-scatter.2.cloned.1.call-update) | async-done | bytes 393232 | tf_op jit(solution)/shard_map/reduce_scatter | solution.py:57
  309.0 0.9 fusion.12
  309.9 33.2 %all-reduce.2.cloned.1.call-done = f32[12,64,128]{2,1,0:T(8,128)} async-done(((f32[12,64,128]{2,1,0:T(8,128)}), f32[12,64,128]{2,1,0:T(8,128)}) %all-reduce.2.cloned.1.call-update) | async-done | bytes 393232 | tf_op jit(solution)/shard_map/psum | solution.py:58
  343.1 1.8 broadcast_multiply_fusion
  (30 shorter events, 3.7 us)
Async XLA Ops:
  7.2 50.3 %copy-start.2 = (s32[1,1,32]{2,1,0:T(1,128)S(1)}, s32[1,1,32]{2,1,0:T(1,128)}, u32[]{:S(2)}) copy-start(s32[1,1,32]{2,1,0:T(1,128)} %param.10) | copy-start | bytes 388
  7.2 49.9 %all-gather.2.cloned.1.call-start = ((), (), s32[]{:S(2)}) async-start(), calls=%async_computation.1 | async-start | bytes 1769472 | tf_op jit(solution)/shard_map/all_gather | solution.py:25
  7.9 301.1 %reduce-scatter.2.cloned.1.call-start = ((), (), s32[]{:S(2)}) async-start(), calls=%async_computation.2 | async-start | bytes 3538944 | tf_op jit(solution)/shard_map/reduce_scatter | solution.py:57
  117.7 1.6 copy-start
  117.7 1.7 copy-start.1
  119.4 223.7 %all-reduce.2.cloned.1.call-start = ((), (), s32[]{:S(2)}) async-start(), calls=%async_computation.3 | async-start | bytes 786432 | tf_op jit(solution)/shard_map/psum | solution.py:58
  119.5 35.6 %collective-permute-start.1 = (bf16[64,1,128]{2,1,0:T(2,128)(2,1)S(1)}, bf16[64,1,128]{2,1,0:T(2,128)(2,1)S(1)}, u32[]{:S(2)}, u32[]{:S(2)}) collective-permute-start(bf16[64,1,128]{2,1,0:T(2,128)(2,1)S(1)} %get-tuple-element.67), channel_id=1, source_target_pairs={{8,0},{16,8},{24,16},{9,1},{17,9},{25,17},{10,2},{18,10},{26,18},{... | collective-permute-start | bytes 49160 | tf_op jit(solution)/shard_map/ppermute | solution.py:15
  120.8 35.1 %collective-permute-start = (bf16[64,1,128]{2,1,0:T(2,128)(2,1)S(1)}, bf16[64,1,128]{2,1,0:T(2,128)(2,1)S(1)}, u32[]{:S(2)}, u32[]{:S(2)}) collective-permute-start(bf16[64,1,128]{2,1,0:T(2,128)(2,1)S(1)} %get-tuple-element.66), channel_id=1, source_target_pairs={{0,8},{8,16},{16,24},{1,9},{9,17},{17,25},{2,10},{10,18},{18,26},{... | collective-permute-start | bytes 49160 | tf_op jit(solution)/shard_map/ppermute | solution.py:14
  156.1 65.1 %collective-permute-start.3 = (bf16[64,6,1]{2,1,0:T(8,128)(2,1)S(1)}, bf16[64,6,1]{2,1,0:T(8,128)(2,1)S(1)}, u32[]{:S(2)}, u32[]{:S(2)}) collective-permute-start(bf16[64,6,1]{2,1,0:T(8,128)(2,1)S(1)} %get-tuple-element.65), channel_id=1, source_target_pairs={{1,0},{2,1},{3,2},{4,3},{5,4},{6,5},{7,6},{9,8},{10,9},{11,10},{12... | collective-permute-start | bytes 2312 | tf_op jit(solution)/shard_map/ppermute | solution.py:15
  157.4 66.4 %collective-permute-start.2 = (bf16[64,6,1]{2,1,0:T(8,128)(2,1)S(1)}, bf16[64,6,1]{2,1,0:T(8,128)(2,1)S(1)}, u32[]{:S(2)}, u32[]{:S(2)}) collective-permute-start(bf16[64,6,1]{2,1,0:T(8,128)(2,1)S(1)} %get-tuple-element.64), channel_id=1, source_target_pairs={{0,1},{1,2},{2,3},{3,4},{4,5},{5,6},{6,7},{8,9},{9,10},{10,11},{11... | collective-permute-start | bytes 2312 | tf_op jit(solution)/shard_map/ppermute | solution.py:14
Sparse Core Ops, SparseCore 0:
  10.2 46.8 all-gather.1
  119.5 189.3 reduce-scatter.1
  311.3 31.7 all-reduce.1
where the time goes:
time: 358 us; the launch traced here: 351 us
  waiting for transfers between devices  171 us (48%)
  starting transfers between devices  99.6 us (28%)
  loops' own time  29.7 us (8%)
  matrix products  24.1 us (7%)
  between operations  13.9 us (4%)
  local copies, waits for them, and re-layouts  9.53 us (3%)
    ppermute x2, starting transfers between devices, extended(): before = lax.ppermute(last, axis, up)  96.9 us
    reduce_scatter x1, waiting for transfers between devices, on_device(): slab = lax.psum_scatter(dense, 'sy', scatter_dimension=0, tiled=True)  84.7 us
    all_gather x1, waiting for transfers between devices, on_device(): factors = lax.all_gather(gene_factors, 'sy', axis=0, tiled=True)  48.3 us
    psum x1, waiting for transfers between devices, on_device(): summed = lax.psum(slab, 'sx')  33.2 us
    another operation x1, loops' own time, on_device(): grad_part, dense = lax.fori_loop(0, live[0, 0], step, (start, dense))  29.7 us
    dot_general x11, matrix products, step(): lax.dot_general(block_factor, wflat, (((0,), (0,)), ((), ())), preferred_...  12.6 us
    dot_general x11, matrix products, step(): lax.dot_general(block_factor, ratio, (((1,), (0,)), ((), ())), preferred_...  9.69 us
  transfers between devices with their start and end apart: 7, of which 6 were waited for; matrix products, arithmetic and copies ran while one was open for 1% of the time, Pallas kernels for 0%

commit v1 on v0

--- a/solution.py
+++ b/solution.py
@@ -1,7 +1,13 @@
+import functools
 import jax
 import jax.numpy as jnp
 from jax import lax
+from jax.experimental import pallas as pl
+from jax.experimental.pallas import tpu as pltpu
 from jax.sharding import PartitionSpec as P
+
+MESH = pl.DeviceIdType.MESH
+GROUP = 4
 
 
 def extended(value, sides, width):
@@ -17,7 +23,7 @@
     return value
 
 
-def on_device(loadings, gene_factors, counts, block_ids, live):
+def by_collectives(loadings, gene_factors, counts, block_ids, live):
     nfac = loadings.shape[0]
     rows = loadings.shape[1]
     cols = loadings.shape[2]
@@ -58,6 +64,254 @@
     summed = lax.psum(slab, "sx")
     grad_genes = summed / (spots * row_count)
     return (grad_loadings, grad_genes)
+
+
+def kernel(nx, ny, rows, ids, inv, live, w, gf, counts, out_l, out_g,
+           facs, cbuf, terms, hl, hr, hu, hd, s_a, r_a, s_b, r_b, s_c, r_c, s_d, r_d,
+           csem, hs, hrs, g1s, g1r, g2s, g2r, g3s, g3r, g4s, g4r,
+           as_, ar, bs, br, cs, cr, ds_, dr):
+    i = lax.axis_index("sx")
+    j = lax.axis_index("sy")
+    x = i // 2
+    c = i % 2
+    sib = x * 2 + (1 - c)
+    opp = (1 - x) * 2 + c
+    diag = (1 - x) * 2 + (1 - c)
+    own = gf.shape[0]
+    q = own // nx
+    cols = w.shape[1] // rows
+    spots = w.shape[1]
+    slots = counts.shape[0]
+    genes = counts.shape[1]
+
+    def remote(src, dst, ss, rs, di, dj):
+        return pltpu.make_async_remote_copy(
+            src_ref=src, dst_ref=dst, send_sem=ss, recv_sem=rs, device_id=(di, dj), device_id_type=MESH
+        )
+
+    load = pltpu.make_async_copy(counts, cbuf, csem)
+    load.start()
+
+    barrier = pltpu.get_barrier_semaphore()
+    for p in (sib, opp, diag):
+        pl.semaphore_signal(barrier, inc=1, device_id=(p, j), device_id_type=MESH)
+    for d in range(1, ny):
+        pl.semaphore_signal(barrier, inc=1, device_id=(i, lax.rem(j + d, ny)), device_id_type=MESH)
+    pl.semaphore_wait(barrier, 3 + ny - 1)
+
+    g1, g2, g3, g4 = [], [], [], []
+    for d in range(1, ny):
+        dst = lax.rem(j + d, ny)
+        g1.append(remote(gf.at[pl.ds(q * i, q)], facs.at[pl.ds(j * own + q * i, q)],
+                         g1s.at[d - 1], g1r.at[d - 1], i, dst))
+        src = lax.rem(j + ny - d, ny)
+        mine = facs.at[pl.ds(src * own + q * i, q)]
+        other = facs.at[pl.ds(src * own + q * opp, q)]
+        g2.append(remote(mine, mine, g2s.at[d - 1], g2r.at[d - 1], opp, j))
+        g3.append(remote(mine, mine, g3s.at[d - 1], g3r.at[d - 1], sib, j))
+        g4.append(remote(other, other, g4s.at[d - 1], g4r.at[d - 1], sib, j))
+    order = sorted(range(ny - 1), key=lambda d: min(d + 1, ny - 1 - d))
+    for d in order[::-1]:
+        g1[d].start()
+    halo = [
+        remote(w, hl, hs.at[0], hrs.at[0], i, lax.rem(j + 1, ny)),
+        remote(w, hr, hs.at[1], hrs.at[1], i, lax.rem(j + ny - 1, ny)),
+        remote(w.at[:, pl.ds((rows - 1) * cols, cols)], hu, hs.at[2], hrs.at[2], lax.rem(i + 1, nx), j),
+        remote(w.at[:, pl.ds(0, cols)], hd, hs.at[3], hrs.at[3], lax.rem(i + nx - 1, nx), j),
+    ]
+    facs[pl.ds(j * own, own)] = gf[...]
+    terms[slots] = jnp.zeros(terms.shape[1:], jnp.float32)
+    out_l[...] = jnp.zeros_like(out_l)
+    for d in order:
+        g1[d].wait_recv()
+        g2[d].start()
+        g3[d].start()
+    for h in halo:
+        h.start()
+    for d in order:
+        g2[d].wait_recv()
+        g4[d].start()
+    for d in order:
+        g3[d].wait_recv()
+        g4[d].wait_recv()
+    load.wait()
+
+    alive = live[0]
+
+    def group(g, _):
+        base = g * GROUP
+        fs = [facs[ids[base + k]] for k in range(GROUP)]
+        f = jnp.concatenate(fs, axis=1)
+        wv = w[...]
+        rate = lax.dot_general(f, wv, (((0,), (0,)), ((), ())), preferred_element_type=jnp.float32)
+        cnt = cbuf[pl.ds(base, GROUP)].reshape(GROUP * genes, spots).astype(jnp.float32)
+        inverse = pl.reciprocal(rate, approx=True)
+        inverse = inverse * (2.0 - rate * inverse)
+        ratio = (1.0 - cnt * inverse).astype(jnp.bfloat16)
+        keep = [jnp.where(base + k < alive, 1.0, 0.0).astype(jnp.float32) for k in range(GROUP)]
+        fm = jnp.concatenate(
+            [(a.astype(jnp.float32) * m).astype(jnp.bfloat16) for a, m in zip(fs, keep)], axis=1
+        )
+        out_l[...] += lax.dot_general(fm, ratio, (((1,), (0,)), ((), ())), preferred_element_type=jnp.float32)
+        term = lax.dot_general(wv, ratio, (((1,), (1,)), ((), ())), preferred_element_type=jnp.float32)
+        for k in range(GROUP):
+            terms[base + k] = term[:, k * genes:(k + 1) * genes]
+        return 0
+
+    lax.fori_loop(0, slots // GROUP, group, 0)
+
+    def owner(t):
+        return lax.rem(j + 1 + t, ny)
+
+    def copy_a(t):
+        return remote(s_a.at[t], r_a.at[t], as_.at[t], ar.at[t], sib, j)
+
+    def copy_b(t):
+        return remote(s_b.at[t], r_b.at[t], bs.at[t], br.at[t], opp, j)
+
+    def copy_c(t):
+        return remote(s_c.at[t], r_c.at[t], cs.at[t], cr.at[t], i, owner(t))
+
+    def stage_a(t, _):
+        for xq in range(2):
+            for k in range(q):
+                b = owner(t) * own + q * (xq * 2 + (1 - c)) + k
+                s_a[t, xq, k] = terms[inv[b]]
+        copy_a(t).start()
+        return 0
+
+    def stage_b(t, _):
+        copy_a(t).wait_recv()
+        for k in range(q):
+            b = owner(t) * own + q * opp + k
+            s_b[t, k] = terms[inv[b]] + r_a[t, 1 - x, k]
+        copy_b(t).start()
+        return 0
+
+    def combine(t):
+        copy_b(t).wait_recv()
+        for k in range(q):
+            b = owner(t) * own + q * i + k
+            s_c[t, k] = terms[inv[b]] + r_a[t, x, k] + r_b[t, k]
+
+    def stage_c(t, _):
+        combine(t)
+        copy_c(t).start()
+        return 0
+
+    lax.fori_loop(0, ny, stage_a, 0)
+    lax.fori_loop(0, ny, stage_b, 0)
+    lax.fori_loop(0, ny - 1, stage_c, 0)
+    combine(ny - 1)
+
+    for h in halo:
+        h.wait()
+    lane = lax.broadcasted_iota(jnp.int32, (w.shape[0], cols), 1)
+    top = jnp.where(i > 0, 1.0, 0.0).astype(jnp.float32)
+    bottom = jnp.where(i < nx - 1, 1.0, 0.0).astype(jnp.float32)
+    west = jnp.where(j > 0, 1.0, 0.0).astype(jnp.float32)
+    east = jnp.where(j < ny - 1, 1.0, 0.0).astype(jnp.float32)
+    parts = [w[:, r * cols:(r + 1) * cols].astype(jnp.float32) for r in range(rows)]
+    for r in range(rows):
+        cut = slice(r * cols, (r + 1) * cols)
+        me = parts[r]
+        up = parts[r - 1] if r > 0 else hu[...].astype(jnp.float32) * top
+        down = parts[r + 1] if r < rows - 1 else hd[...].astype(jnp.float32) * bottom
+        lnb = hl[:, cut].astype(jnp.float32) * west
+        rnb = hr[:, cut].astype(jnp.float32) * east
+        left = pltpu.roll(jnp.where(lane == cols - 1, lnb, me), 1, 1)
+        right = pltpu.roll(jnp.where(lane == 0, rnb, me), cols - 1, 1)
+        out_l[:, cut] += 0.5 * (4.0 * me - (down + up + right + left))
+
+    total = s_c[ny - 1]
+    for t in range(ny - 1):
+        copy_c(t).wait_recv()
+        total = total + r_c[t]
+    total = total / (spots * nx)
+    s_d[...] = total
+    peers = (sib, opp, diag)
+    share = [remote(s_d, r_d.at[p], ds_.at[p], dr.at[p], peers[p], j) for p in range(3)]
+    for p in (1, 2, 0):
+        share[p].start()
+    out_g[pl.ds(q * i, q)] = total
+    for p in range(3):
+        share[p].wait_recv()
+        out_g[pl.ds(q * peers[p], q)] = r_d[p]
+    for p in range(3):
+        share[p].wait_send()
+    for d in range(ny - 1):
+        g1[d].wait_send()
+        g2[d].wait_send()
+        g3[d].wait_send()
+        g4[d].wait_send()
+
+    def drain(t, _):
+        copy_a(t).wait_send()
+        copy_b(t).wait_send()
+        return 0
+
+    def drain_c(t, _):
+        copy_c(t).wait_send()
+        return 0
+
+    lax.fori_loop(0, ny, drain, 0)
+    lax.fori_loop(0, ny - 1, drain_c, 0)
+
+
+def by_kernel(loadings, gene_factors, counts, block_ids, live):
+    nfac, rows, cols = loadings.shape
+    spots = rows * cols
+    nx, ny = lax.axis_size("sx"), lax.axis_size("sy")
+    own, _, genes = gene_factors.shape
+    slots = counts.shape[2]
+    q = own // nx
+    ids = block_ids[0, 0]
+    slot = jnp.arange(slots, dtype=jnp.int32)
+    hit = (ids[None, :] == jnp.arange(own * ny, dtype=jnp.int32)[:, None]) & (slot < live[0, 0])[None, :]
+    inv = jnp.min(jnp.where(hit, slot[None, :], slots), axis=1).astype(jnp.int32)
+    dma = pltpu.SemaphoreType.DMA
+    f32, bf16 = jnp.float32, jnp.bfloat16
+    smem = pl.BlockSpec(memory_space=pltpu.SMEM)
+    vmem = pl.BlockSpec(memory_space=pltpu.VMEM)
+    grad_l, grad_g = pl.pallas_call(
+        functools.partial(kernel, nx, ny, rows),
+        out_shape=(
+            jax.ShapeDtypeStruct((nfac, spots), f32),
+            jax.ShapeDtypeStruct((own, nfac, genes), f32),
+        ),
+        in_specs=[smem, smem, smem, vmem, vmem, pl.BlockSpec(memory_space=pl.ANY)],
+        out_specs=(vmem, vmem),
+        scratch_shapes=[
+            pltpu.VMEM((ny * own, nfac, genes), bf16),
+            pltpu.VMEM((slots, genes, spots), bf16),
+            pltpu.VMEM((slots + 1, nfac, genes), f32),
+            pltpu.VMEM((nfac, spots), bf16),
+            pltpu.VMEM((nfac, spots), bf16),
+            pltpu.VMEM((nfac, cols), bf16),
+            pltpu.VMEM((nfac, cols), bf16),
+            pltpu.VMEM((ny, 2, q, nfac, genes), f32),
+            pltpu.VMEM((ny, 2, q, nfac, genes), f32),
+            pltpu.VMEM((ny, q, nfac, genes), f32),
+            pltpu.VMEM((ny, q, nfac, genes), f32),
+            pltpu.VMEM((ny, q, nfac, genes), f32),
+            pltpu.VMEM((ny - 1, q, nfac, genes), f32),
+            pltpu.VMEM((q, nfac, genes), f32),
+            pltpu.VMEM((3, q, nfac, genes), f32),
+            dma, dma((4,)), dma((4,)),
+        ] + [dma((ny - 1,))] * 8 + [dma((ny,))] * 4 + [dma((ny - 1,))] * 2 + [dma((3,))] * 2,
+        compiler_params=pltpu.CompilerParams(
+            collective_id=0, has_side_effects=True, vmem_limit_bytes=40 * 1024 * 1024
+        ),
+    )(ids, inv, live[0], loadings.reshape(nfac, spots), gene_factors, counts[0, 0])
+    return grad_l.reshape(nfac, rows, cols), grad_g
+
+
+def on_device(loadings, gene_factors, counts, block_ids, live):
+    nx, ny = lax.axis_size("sx"), lax.axis_size("sy")
+    fits = nx == 4 and ny > 1 and gene_factors.shape[0] % nx == 0
+    fits = fits and loadings.shape[2] % 128 == 0 and counts.shape[2] % GROUP == 0
+    form = by_kernel if fits else by_collectives
+    return form(loadings, gene_factors, counts, block_ids, live)
 
 
 def solution(mesh):

time: 358 us -> 67.4 us (0.19)
  the two profiles are of different devices: /device:TPU:0 before, /device:TPU:29 now
where the time goes in v1:
time: 67.4 us; the launch traced here: 67.1 us
  Pallas kernels  59 us (88%)
  local copies, waits for them, and re-layouts  6.06 us (9%)
  between operations  1.31 us (2%)
  other arithmetic  0.75 us (1%)
    pallas_call x1, Pallas kernels, by_kernel(): pl.pallas_call(functools.partial(kernel, nx, ny, rows), out_shape=(jax.Sh...  59 us
    unnamed x8, local copies, waits for them, and re-layouts  5.36 us

profile of v1, /device:TPU:29, one launch (start us, length us, event | category | flops | bytes accessed | tf_op | source)
XLA Modules:
  0.0 67.1 jit_solution(5571366170649520168)
XLA Ops:
  1.3 0.7 %select_reduce_fusion.inv = s32[96]{0:T(128)S(1)} fusion(s32[32]{0:T(128)} %bitcast.12, pred[32]{0:T(512)(128)(4,1)S(1)} %iota_compare_fusion.1), kind=kLoop, calls=%fused_computation.1 | loop fusion | flops 12192 | bytes 544 | tf_op jit(solution)/shard_map/reduce_min | solution.py:271
  2.0 0.9 %copy.9 = bf16[8,8,4,128]{3,1,2,0:T(8,128)(2,1)S(1)} copy(bf16[8,8,4,128]{3,2,1,0:T(4,128)(2,1)} %bitcast.14) | data formatting | bytes 131072
  2.9 0.0 copy-start
  2.9 2.2 %copy-done = bf16[1,1,32,128,512]{4,3,2,1,0:T(8,128)(2,1)S(1)} copy-done((bf16[1,1,32,128,512]{4,3,2,1,0:T(8,128)(2,1)S(1)}, bf16[1,1,32,128,512]{4,3,2,1,0:T(8,128)(2,1)}, u32[]{:S(2)}) %copy-start) | copy-done | bytes 4194328
  5.1 0.0 copy-start.1
  5.1 0.9 %copy-done.1 = bf16[12,64,128]{2,1,0:T(8,128)(2,1)S(1)} copy-done((bf16[12,64,128]{2,1,0:T(8,128)(2,1)S(1)}, bf16[12,64,128]{2,1,0:T(8,128)(2,1)}, u32[]{:S(2)}) %copy-start.1) | copy-done | bytes 196632
  6.0 0.0 copy-start.2
  6.0 0.7 copy-done.2
  6.7 59.0 %shard_map.68 = (f32[64,512]{1,0:T(8,128)S(1)}, f32[12,64,128]{2,1,0:T(8,128)S(1)}) custom-call(s32[32]{0:T(128)S(1)} %bitcast.13, s32[96]{0:T(128)S(1)} %select_reduce_fusion.inv, s32[1]{0:T(128)} %bitcast.9.live, bf16[64,512]{1,0:T(8,128)(2,1)S(1)} %bitcast.11, bf16[12,64,128]{2,1,0:T(8,128)(2,1)S(1)} %copy-done.1, bf16[32,128,512]{2,1,0:T(8,128)(2,1)S(1)} %bitcast.10), custom_call_target="tpu_custom_call" | custom-call | tf_op jit(solution)/shard_map/pallas_call | solution.py:276
  65.7 0.7 %reshape.16 = f32[64,4,128]{2,1,0:T(4,128)} reshape(f32[64,512]{1,0:T(8,128)S(1)} %get-tuple-element.4) | data formatting | bytes 262144 | tf_op jit(solution)/shard_map/reshape | solution.py:306
  66.4 0.7 %copy.12 = f32[12,64,128]{2,1,0:T(8,128)} copy(f32[12,64,128]{2,1,0:T(8,128)S(1)} %get-tuple-element.9) | data formatting | bytes 786432
  (1 shorter events, 0.0 us)
Async XLA Ops:
  2.9 2.2 %copy-start = (bf16[1,1,32,128,512]{4,3,2,1,0:T(8,128)(2,1)S(1)}, bf16[1,1,32,128,512]{4,3,2,1,0:T(8,128)(2,1)}, u32[]{:S(2)}) copy-start(bf16[1,1,32,128,512]{4,3,2,1,0:T(8,128)(2,1)} %param.7) | copy-start | bytes 12582916
  5.1 0.9 %copy-start.1 = (bf16[12,64,128]{2,1,0:T(8,128)(2,1)S(1)}, bf16[12,64,128]{2,1,0:T(8,128)(2,1)}, u32[]{:S(2)}) copy-start(bf16[12,64,128]{2,1,0:T(8,128)(2,1)} %gf.1) | copy-start | bytes 589828
  6.0 0.7 copy-start.2

commit v2 on v1

--- a/solution.py
+++ b/solution.py
@@ -67,73 +67,107 @@
 
 
 def kernel(nx, ny, rows, ids, inv, live, w, gf, counts, out_l, out_g,
-           facs, cbuf, terms, hl, hr, hu, hd, s_a, r_a, s_b, r_b, s_c, r_c, s_d, r_d,
-           csem, hs, hrs, g1s, g1r, g2s, g2r, g3s, g3r, g4s, g4r,
-           as_, ar, bs, br, cs, cr, ds_, dr):
+           facs, cbuf, terms, hl, hr, hu, hd, s_a, r_a, s_b, r_b, s_c, r_c, s_d, r_d, s_e, r_e,
+           csem, fsem, hs, hrs, ga, gar, gb, gbr, gc, gcr, gd, gdr,
+           as_, ar, bs, br, cs, cr, ds_, dr, es, er):
     i = lax.axis_index("sx")
     j = lax.axis_index("sy")
-    x = i // 2
-    c = i % 2
+    x, c = i // 2, i % 2
+    z, y = j // 2, j % 2
     sib = x * 2 + (1 - c)
     opp = (1 - x) * 2 + c
     diag = (1 - x) * 2 + (1 - c)
+    nz = ny // 2
     own = gf.shape[0]
     q = own // nx
     cols = w.shape[1] // rows
     spots = w.shape[1]
     slots = counts.shape[0]
     genes = counts.shape[1]
+    u, v = x * (1 - c) + y * c, y * (1 - c) + x * c
+    zs = [lax.rem(z + 2, nz), nz - 1 - z, z + 1 - 2 * (z % 2), z]
+
+    def at(uu, vv):
+        return uu * (1 - c) + vv * c, vv * (1 - c) + uu * c
 
     def remote(src, dst, ss, rs, di, dj):
         return pltpu.make_async_remote_copy(
             src_ref=src, dst_ref=dst, send_sem=ss, recv_sem=rs, device_id=(di, dj), device_id_type=MESH
         )
 
-    load = pltpu.make_async_copy(counts, cbuf, csem)
-    load.start()
+    def to(src, dst, ss, rs, uu, vv, zz):
+        xx, yy = at(uu, vv)
+        return remote(src, dst, ss, rs, xx * 2 + c, zz * 2 + yy)
+
+    def first(uu, vv, zz):
+        xx, yy = at(uu, vv)
+        return (zz * 2 + yy) * own + q * (xx * 2 + c)
 
     barrier = pltpu.get_barrier_semaphore()
     for p in (sib, opp, diag):
         pl.semaphore_signal(barrier, inc=1, device_id=(p, j), device_id_type=MESH)
     for d in range(1, ny):
         pl.semaphore_signal(barrier, inc=1, device_id=(i, lax.rem(j + d, ny)), device_id_type=MESH)
+    mine = pl.ds(j * own + q * i, q)
+    fetch = pltpu.make_async_copy(gf.at[pl.ds(q * i, q)], facs.at[mine], fsem)
+    fetch.start()
+    load = pltpu.make_async_copy(counts, cbuf, csem)
+    load.start()
+    terms[slots] = jnp.zeros(terms.shape[1:], jnp.float32)
+    out_l[...] = jnp.zeros_like(out_l)
+    fetch.wait()
     pl.semaphore_wait(barrier, 3 + ny - 1)
 
-    g1, g2, g3, g4 = [], [], [], []
-    for d in range(1, ny):
-        dst = lax.rem(j + d, ny)
-        g1.append(remote(gf.at[pl.ds(q * i, q)], facs.at[pl.ds(j * own + q * i, q)],
-                         g1s.at[d - 1], g1r.at[d - 1], i, dst))
-        src = lax.rem(j + ny - d, ny)
-        mine = facs.at[pl.ds(src * own + q * i, q)]
-        other = facs.at[pl.ds(src * own + q * opp, q)]
-        g2.append(remote(mine, mine, g2s.at[d - 1], g2r.at[d - 1], opp, j))
-        g3.append(remote(mine, mine, g3s.at[d - 1], g3r.at[d - 1], sib, j))
-        g4.append(remote(other, other, g4s.at[d - 1], g4r.at[d - 1], sib, j))
-    order = sorted(range(ny - 1), key=lambda d: min(d + 1, ny - 1 - d))
-    for d in order[::-1]:
-        g1[d].start()
+    last = nz - 1
+    cd, cc, cb, ca = {}, {}, {}, {}
+    for t in range(nz):
+        p0 = facs.at[pl.ds(first(u, v, zs[t]), q)]
+        p1 = facs.at[pl.ds(first(u, 1 - v, zs[t]), q)]
+        p2 = facs.at[pl.ds(first(1 - u, v, zs[t]), q)]
+        p3 = facs.at[pl.ds(first(1 - u, 1 - v, zs[t]), q)]
+        if t < last:
+            own_piece = facs.at[mine]
+            cd[t] = to(own_piece, own_piece, gd.at[t], gdr.at[t], u, v, zs[t])
+        cc[t] = to(p0, p0, gc.at[t], gcr.at[t], u, 1 - v, z)
+        cb[t, 1] = to(p0, p0, gb.at[t, 1], gbr.at[t, 0 + 1], 1 - u, v, z)
+        cb[t, 0] = to(p1, p1, gb.at[t, 0], gbr.at[t, 0], 1 - u, v, z)
+        for e, piece in enumerate((p0, p1, p2, p3)):
+            ca[t, e] = remote(piece, piece, ga.at[t, e], gar.at[t, e], sib, j)
+
+    def have(t):
+        cb[t, 1].start()
+        cc[t].start()
+        ca[t, 0].start()
+
+    def got_d(t):
+        cd[t].wait_recv()
+        have(t)
+
+    def got_c(t):
+        cc[t].wait_recv()
+        cb[t, 0].start()
+        ca[t, 1].start()
+
+    def got_b(t, e):
+        cb[t, e].wait_recv()
+        ca[t, 3 - e].start()
+
+    for t in range(last):
+        cd[t].start()
+    have(last)
+    got_c(3), got_d(2), got_b(3, 1), got_d(1), got_c(2), got_d(0), got_b(3, 0), got_b(2, 1), got_c(1)
+    got_b(2, 0), got_b(1, 1), got_c(0), got_b(1, 0), got_b(0, 1), got_b(0, 0)
     halo = [
         remote(w, hl, hs.at[0], hrs.at[0], i, lax.rem(j + 1, ny)),
         remote(w, hr, hs.at[1], hrs.at[1], i, lax.rem(j + ny - 1, ny)),
         remote(w.at[:, pl.ds((rows - 1) * cols, cols)], hu, hs.at[2], hrs.at[2], lax.rem(i + 1, nx), j),
         remote(w.at[:, pl.ds(0, cols)], hd, hs.at[3], hrs.at[3], lax.rem(i + nx - 1, nx), j),
     ]
-    facs[pl.ds(j * own, own)] = gf[...]
-    terms[slots] = jnp.zeros(terms.shape[1:], jnp.float32)
-    out_l[...] = jnp.zeros_like(out_l)
-    for d in order:
-        g1[d].wait_recv()
-        g2[d].start()
-        g3[d].start()
     for h in halo:
         h.start()
-    for d in order:
-        g2[d].wait_recv()
-        g4[d].start()
-    for d in order:
-        g3[d].wait_recv()
-        g4[d].wait_recv()
+    for t in range(nz):
+        for e in range(4):
+            ca[t, e].wait_recv()
     load.wait()
 
     alive = live[0]
@@ -160,49 +194,52 @@
 
     lax.fori_loop(0, slots // GROUP, group, 0)
 
-    def owner(t):
-        return lax.rem(j + 1 + t, ny)
-
-    def copy_a(t):
-        return remote(s_a.at[t], r_a.at[t], as_.at[t], ar.at[t], sib, j)
-
-    def copy_b(t):
-        return remote(s_b.at[t], r_b.at[t], bs.at[t], br.at[t], opp, j)
-
-    def copy_c(t):
-        return remote(s_c.at[t], r_c.at[t], cs.at[t], cr.at[t], i, owner(t))
-
-    def stage_a(t, _):
-        for xq in range(2):
+    a_, b_, c_, d_ = {}, {}, {}, {}
+    for t in range(nz):
+        a_[t] = remote(s_a.at[t], r_a.at[t], as_.at[t], ar.at[t], sib, j)
+        for e in range(2):
+            b_[t, e] = to(s_b.at[t, e], r_b.at[t, e], bs.at[t, e], br.at[t, e], 1 - u, v, z)
+        c_[t] = to(s_c.at[t], r_c.at[t], cs.at[t], cr.at[t], u, 1 - v, z)
+        if t < last:
+            d_[t] = to(s_d.at[t], r_d.at[t], ds_.at[t], dr.at[t], u, v, zs[t])
+
+    for t in range(nz):
+        for xx in range(2):
+            for yy in range(2):
+                for k in range(q):
+                    b = (zs[t] * 2 + yy) * own + q * (xx * 2 + (1 - c)) + k
+                    s_a[t, xx, yy, k] = terms[inv[b]]
+        a_[t].start()
+
+    def partial(t, uu, vv, k):
+        xx, yy = at(uu, vv)
+        return terms[inv[first(uu, vv, zs[t]) + k]] + r_a[t, xx, yy, k]
+
+    for t in range(nz):
+        a_[t].wait_recv()
+        for e in range(2):
             for k in range(q):
-                b = owner(t) * own + q * (xq * 2 + (1 - c)) + k
-                s_a[t, xq, k] = terms[inv[b]]
-        copy_a(t).start()
-        return 0
-
-    def stage_b(t, _):
-        copy_a(t).wait_recv()
+                s_b[t, e, k] = partial(t, 1 - u, v if e else 1 - v, k)
+            b_[t, e].start()
+
+    def stage_c(t):
+        b_[t, 0].wait_recv()
         for k in range(q):
-            b = owner(t) * own + q * opp + k
-            s_b[t, k] = terms[inv[b]] + r_a[t, 1 - x, k]
-        copy_b(t).start()
-        return 0
-
-    def combine(t):
-        copy_b(t).wait_recv()
+            s_c[t, k] = partial(t, u, 1 - v, k) + r_b[t, 0, k]
+        c_[t].start()
+
+    def stage_d(t):
+        b_[t, 1].wait_recv()
+        c_[t].wait_recv()
         for k in range(q):
-            b = owner(t) * own + q * i + k
-            s_c[t, k] = terms[inv[b]] + r_a[t, x, k] + r_b[t, k]
-
-    def stage_c(t, _):
-        combine(t)
-        copy_c(t).start()
-        return 0
-
-    lax.fori_loop(0, ny, stage_a, 0)
-    lax.fori_loop(0, ny, stage_b, 0)
-    lax.fori_loop(0, ny - 1, stage_c, 0)
-    combine(ny - 1)
+            s_d[t, k] = partial(t, u, v, k) + r_b[t, 1, k] + r_c[t, k]
+        if t < last:
+            d_[t].start()
+
+    stage_c(0)
+    for t in range(1, nz):
+        stage_c(t)
+        stage_d(t - 1)
 
     for h in halo:
         h.wait()
@@ -223,39 +260,37 @@
         right = pltpu.roll(jnp.where(lane == 0, rnb, me), cols - 1, 1)
         out_l[:, cut] += 0.5 * (4.0 * me - (down + up + right + left))
 
-    total = s_c[ny - 1]
-    for t in range(ny - 1):
-        copy_c(t).wait_recv()
-        total = total + r_c[t]
-    total = total / (spots * nx)
-    s_d[...] = total
-    peers = (sib, opp, diag)
-    share = [remote(s_d, r_d.at[p], ds_.at[p], dr.at[p], peers[p], j) for p in range(3)]
-    for p in (1, 2, 0):
-        share[p].start()
-    out_g[pl.ds(q * i, q)] = total
-    for p in range(3):
-        share[p].wait_recv()
-        out_g[pl.ds(q * peers[p], q)] = r_d[p]
-    for p in range(3):
-        share[p].wait_send()
-    for d in range(ny - 1):
-        g1[d].wait_send()
-        g2[d].wait_send()
-        g3[d].wait_send()
-        g4[d].wait_send()
-
-    def drain(t, _):
-        copy_a(t).wait_send()
-        copy_b(t).wait_send()
-        return 0
-
-    def drain_c(t, _):
-        copy_c(t).wait_send()
-        return 0
-
-    lax.fori_loop(0, ny, drain, 0)
-    lax.fori_loop(0, ny - 1, drain_c, 0)
+    stage_d(last)
+    for t in range(last):
+        d_[t].wait_recv()
+    near, over, pass_on = [], [], []
+    for k in range(q):
+        total = s_d[last, k]
+        for t in range(last):
+            total = total + r_d[t, k]
+        total = total / (spots * nx)
+        s_e[k] = total
+        over.append(remote(s_e.at[k], r_e.at[0, k], es.at[0, k], er.at[0, k], opp, j))
+        near.append(remote(s_e.at[k], r_e.at[1, k], es.at[1, k], er.at[1, k], sib, j))
+        pass_on.append(remote(r_e.at[0, k], r_e.at[2, k], es.at[2, k], er.at[2, k], sib, j))
+        over[k].start()
+        near[k].start()
+        out_g[q * i + k] = total
+    for k in range(q):
+        over[k].wait_recv()
+        pass_on[k].start()
+        out_g[q * opp + k] = r_e[0, k]
+    for k in range(q):
+        near[k].wait_recv()
+        out_g[q * sib + k] = r_e[1, k]
+    for k in range(q):
+        pass_on[k].wait_recv()
+        out_g[q * diag + k] = r_e[2, k]
+    for group_of in (cd, cc, cb, ca, a_, b_, c_, d_):
+        for copy in group_of.values():
+            copy.wait_send()
+    for copy in over + near + pass_on:
+        copy.wait_send()
 
 
 def by_kernel(loadings, gene_factors, counts, block_ids, live):
@@ -265,6 +300,7 @@
     own, _, genes = gene_factors.shape
     slots = counts.shape[2]
     q = own // nx
+    nz = ny // 2
     ids = block_ids[0, 0]
     slot = jnp.arange(slots, dtype=jnp.int32)
     hit = (ids[None, :] == jnp.arange(own * ny, dtype=jnp.int32)[:, None]) & (slot < live[0, 0])[None, :]
@@ -279,7 +315,7 @@
             jax.ShapeDtypeStruct((nfac, spots), f32),
             jax.ShapeDtypeStruct((own, nfac, genes), f32),
         ),
-        in_specs=[smem, smem, smem, vmem, vmem, pl.BlockSpec(memory_space=pl.ANY)],
+        in_specs=[smem, smem, smem, vmem] + [pl.BlockSpec(memory_space=pl.ANY)] * 2,
         out_specs=(vmem, vmem),
         scratch_shapes=[
             pltpu.VMEM((ny * own, nfac, genes), bf16),
@@ -289,18 +325,22 @@
             pltpu.VMEM((nfac, spots), bf16),
             pltpu.VMEM((nfac, cols), bf16),
             pltpu.VMEM((nfac, cols), bf16),
-            pltpu.VMEM((ny, 2, q, nfac, genes), f32),
-            pltpu.VMEM((ny, 2, q, nfac, genes), f32),
-            pltpu.VMEM((ny, q, nfac, genes), f32),
-            pltpu.VMEM((ny, q, nfac, genes), f32),
-            pltpu.VMEM((ny, q, nfac, genes), f32),
-            pltpu.VMEM((ny - 1, q, nfac, genes), f32),
+            pltpu.VMEM((nz, 2, 2, q, nfac, genes), f32),
+            pltpu.VMEM((nz, 2, 2, q, nfac, genes), f32),
+            pltpu.VMEM((nz, 2, q, nfac, genes), f32),
+            pltpu.VMEM((nz, 2, q, nfac, genes), f32),
+            pltpu.VMEM((nz, q, nfac, genes), f32),
+            pltpu.VMEM((nz, q, nfac, genes), f32),
+            pltpu.VMEM((nz, q, nfac, genes), f32),
+            pltpu.VMEM((nz - 1, q, nfac, genes), f32),
             pltpu.VMEM((q, nfac, genes), f32),
             pltpu.VMEM((3, q, nfac, genes), f32),
-            dma, dma((4,)), dma((4,)),
-        ] + [dma((ny - 1,))] * 8 + [dma((ny,))] * 4 + [dma((ny - 1,))] * 2 + [dma((3,))] * 2,
+            dma, dma, dma((4,)), dma((4,)),
+        ] + [dma((nz, 4))] * 2 + [dma((nz, 2))] * 2 + [dma((nz,))] * 2 + [dma((nz - 1,))] * 2
+        + [dma((nz,))] * 2 + [dma((nz, 2))] * 2 + [dma((nz,))] * 2 + [dma((nz - 1,))] * 2
+        + [dma((3, q))] * 2,
         compiler_params=pltpu.CompilerParams(
-            collective_id=0, has_side_effects=True, vmem_limit_bytes=40 * 1024 * 1024
+            collective_id=0, has_side_effects=True, vmem_limit_bytes=60 * 1024 * 1024
         ),
     )(ids, inv, live[0], loadings.reshape(nfac, spots), gene_factors, counts[0, 0])
     return grad_l.reshape(nfac, rows, cols), grad_g
@@ -308,7 +348,7 @@
 
 def on_device(loadings, gene_factors, counts, block_ids, live):
     nx, ny = lax.axis_size("sx"), lax.axis_size("sy")
-    fits = nx == 4 and ny > 1 and gene_factors.shape[0] % nx == 0
+    fits = nx == 4 and ny == 8 and gene_factors.shape[0] % nx == 0
     fits = fits and loadings.shape[2] % 128 == 0 and counts.shape[2] % GROUP == 0
     form = by_kernel if fits else by_collectives
     return form(loadings, gene_factors, counts, block_ids, live)

time: 67.4 us -> 62.2 us (0.923)
  the two profiles are of different devices: /device:TPU:29 before, /device:TPU:0 now
where the time goes in v2:
time: 62.2 us; the launch traced here: 61.9 us
  Pallas kernels  54.4 us (87%)
  local copies, waits for them, and re-layouts  4.85 us (8%)
  other arithmetic  1.35 us (2%)
  between operations  1.29 us (2%)
    pallas_call x1, Pallas kernels, by_kernel(): pl.pallas_call(functools.partial(kernel, nx, ny, rows), out_shape=(jax.Sh...  54.4 us
    unnamed x2, local copies, waits for them, and re-layouts  3.24 us
    reshape x1, local copies, waits for them, and re-layouts, by_kernel(): return (grad_l.reshape(nfac, rows, cols), grad_g)  1.6 us
    reduce_min x1, other arithmetic, by_kernel(): jnp.min(jnp.where(hit, slot[None, :], slots), axis=1).astype(jnp.int32)  1.34 us

profile of v2, /device:TPU:0, one launch (start us, length us, event | category | flops | bytes accessed | tf_op | source)
XLA Modules:
  0.0 61.9 jit_solution(2271166744895726046)
XLA Ops:
  1.3 1.3 %select_reduce_fusion.inv = s32[96]{0:T(128)} fusion(s32[32]{0:T(128)} %bitcast.13, pred[32]{0:T(512)(128)(4,1)S(1)} %iota_compare_fusion.1), kind=kLoop, calls=%fused_computation.1 | loop fusion | flops 12192 | bytes 544 | tf_op jit(solution)/shard_map/reduce_min | solution.py:307
  2.6 1.5 %copy.9 = bf16[8,8,4,128]{3,1,2,0:T(8,128)(2,1)} copy(bf16[8,8,4,128]{3,2,1,0:T(4,128)(2,1)} %bitcast.12) | data formatting | bytes 131072
  4.1 54.4 %shard_map.68 = (f32[64,512]{1,0:T(8,128)}, f32[12,64,128]{2,1,0:T(8,128)}) custom-call(s32[32]{0:T(128)} %bitcast.14, s32[96]{0:T(128)} %select_reduce_fusion.inv, s32[1]{0:T(128)} %bitcast.9.live, bf16[64,512]{1,0:T(8,128)(2,1)} %bitcast.11, bf16[12,64,128]{2,1,0:T(8,128)(2,1)} %gf.1, bf16[32,128,512]{2,1,0:T(8,128)(2,1)} %bitcast.10), custom_call_target="tpu_custom_call" | custom-call | tf_op jit(solution)/shard_map/pallas_call | solution.py:312
  58.5 1.6 %reshape.16 = f32[64,4,128]{2,1,0:T(4,128)} reshape(f32[64,512]{1,0:T(8,128)} %get-tuple-element.4) | data formatting | bytes 262144 | tf_op jit(solution)/shard_map/reshape | solution.py:346
  60.1 1.8 %copy.12 = f32[12,64,128]{2,1,0:T(8,128)} copy(f32[12,64,128]{2,1,0:T(8,128)} %get-tuple-element.9) | data formatting | bytes 786432
  (1 shorter events, 0.0 us)

commit v3 on v2

--- a/solution.py
+++ b/solution.py
@@ -64,6 +64,23 @@
     summed = lax.psum(slab, "sx")
     grad_genes = summed / (spots * row_count)
     return (grad_loadings, grad_genes)
+
+
+def encode(dst, values):
+    top = functools.reduce(jnp.maximum, [jnp.max(jnp.abs(a), axis=0, keepdims=True) for a in values])
+    power = jnp.floor(jnp.log2(jnp.maximum(top, 1e-30))) - 13.0
+    factor = jnp.exp2(-power)
+    n = values[0].shape[0]
+    for k, a in enumerate(values):
+        dst[k * n:(k + 1) * n] = jnp.floor(a * factor + 0.5).astype(jnp.int32).astype(jnp.int16)
+    tail = jnp.broadcast_to(power.astype(jnp.int32), (16, top.shape[1]))
+    dst[len(values) * n:len(values) * n + 16] = tail.astype(jnp.int16)
+
+
+def decode(src, count, n):
+    power = src[count * n:count * n + 16].astype(jnp.int32).astype(jnp.float32)
+    factor = jnp.exp2(power[0:1])
+    return [src[k * n:(k + 1) * n].astype(jnp.int32).astype(jnp.float32) * factor for k in range(count)]
 
 
 def kernel(nx, ny, rows, ids, inv, live, w, gf, counts, out_l, out_g,
@@ -84,6 +101,7 @@
     spots = w.shape[1]
     slots = counts.shape[0]
     genes = counts.shape[1]
+    nfac = w.shape[0]
     u, v = x * (1 - c) + y * c, y * (1 - c) + x * c
     zs = [lax.rem(z + 2, nz), nz - 1 - z, z + 1 - 2 * (z % 2), z]
 
@@ -218,21 +236,21 @@
     for t in range(nz):
         a_[t].wait_recv()
         for e in range(2):
-            for k in range(q):
-                s_b[t, e, k] = partial(t, 1 - u, v if e else 1 - v, k)
+            encode(s_b.at[t, e], [partial(t, 1 - u, v if e else 1 - v, k) for k in range(q)])
             b_[t, e].start()
 
     def stage_c(t):
         b_[t, 0].wait_recv()
-        for k in range(q):
-            s_c[t, k] = partial(t, u, 1 - v, k) + r_b[t, 0, k]
+        came = decode(r_b.at[t, 0], q, nfac)
+        encode(s_c.at[t], [partial(t, u, 1 - v, k) + came[k] for k in range(q)])
         c_[t].start()
 
     def stage_d(t):
         b_[t, 1].wait_recv()
         c_[t].wait_recv()
+        came, more = decode(r_b.at[t, 1], q, nfac), decode(r_c.at[t], q, nfac)
         for k in range(q):
-            s_d[t, k] = partial(t, u, v, k) + r_b[t, 1, k] + r_c[t, k]
+            s_d[t, k] = partial(t, u, v, k) + came[k] + more[k]
         if t < last:
             d_[t].start()
 
@@ -327,10 +345,10 @@
             pltpu.VMEM((nfac, cols), bf16),
             pltpu.VMEM((nz, 2, 2, q, nfac, genes), f32),
             pltpu.VMEM((nz, 2, 2, q, nfac, genes), f32),
-            pltpu.VMEM((nz, 2, q, nfac, genes), f32),
-            pltpu.VMEM((nz, 2, q, nfac, genes), f32),
-            pltpu.VMEM((nz, q, nfac, genes), f32),
-            pltpu.VMEM((nz, q, nfac, genes), f32),
+            pltpu.VMEM((nz, 2, q * nfac + 16, genes), jnp.int16),
+            pltpu.VMEM((nz, 2, q * nfac + 16, genes), jnp.int16),
+            pltpu.VMEM((nz, q * nfac + 16, genes), jnp.int16),
+            pltpu.VMEM((nz, q * nfac + 16, genes), jnp.int16),
             pltpu.VMEM((nz, q, nfac, genes), f32),
             pltpu.VMEM((nz - 1, q, nfac, genes), f32),
             pltpu.VMEM((q, nfac, genes), f32),

time: 62.2 us -> 58.4 us (0.939)
  Pallas kernels: 54.4 us -> 50.7 us
    pallas_call x1, Pallas kernels: 54.4 us -> 50.7 us  [by_kernel(): pl.pallas_call(functools.partial(kernel, nx, ny, rows), out_shape=(jax.Sh...]
where the time goes in v3:
time: 58.4 us; the launch traced here: 58.1 us
  Pallas kernels  50.7 us (87%)
  local copies, waits for them, and re-layouts  4.85 us (8%)
  other arithmetic  1.35 us (2%)
  between operations  1.29 us (2%)
    pallas_call x1, Pallas kernels, by_kernel(): pl.pallas_call(functools.partial(kernel, nx, ny, rows), out_shape=(jax.Sh...  50.7 us
    unnamed x2, local copies, waits for them, and re-layouts  3.24 us
    reshape x1, local copies, waits for them, and re-layouts, by_kernel(): return (grad_l.reshape(nfac, rows, cols), grad_g)  1.6 us
    reduce_min x1, other arithmetic, by_kernel(): jnp.min(jnp.where(hit, slot[None, :], slots), axis=1).astype(jnp.int32)  1.34 us

profile of v3, /device:TPU:0, one launch (start us, length us, event | category | flops | bytes accessed | tf_op | source)
XLA Modules:
  0.0 58.1 jit_solution(10553179286301069766)
XLA Ops:
  1.3 1.3 %select_reduce_fusion.inv = s32[96]{0:T(128)} fusion(s32[32]{0:T(128)} %bitcast.13, pred[32]{0:T(512)(128)(4,1)S(1)} %iota_compare_fusion.1), kind=kLoop, calls=%fused_computation.1 | loop fusion | flops 12192 | bytes 544 | tf_op jit(solution)/shard_map/reduce_min | solution.py:325
  2.6 1.5 %copy.9 = bf16[8,8,4,128]{3,1,2,0:T(8,128)(2,1)} copy(bf16[8,8,4,128]{3,2,1,0:T(4,128)(2,1)} %bitcast.12) | data formatting | bytes 131072
  4.1 50.7 %shard_map.68 = (f32[64,512]{1,0:T(8,128)}, f32[12,64,128]{2,1,0:T(8,128)}) custom-call(s32[32]{0:T(128)} %bitcast.14, s32[96]{0:T(128)} %select_reduce_fusion.inv, s32[1]{0:T(128)} %bitcast.9.live, bf16[64,512]{1,0:T(8,128)(2,1)} %bitcast.11, bf16[12,64,128]{2,1,0:T(8,128)(2,1)} %gf.1, bf16[32,128,512]{2,1,0:T(8,128)(2,1)} %bitcast.10), custom_call_target="tpu_custom_call" | custom-call | tf_op jit(solution)/shard_map/pallas_call | solution.py:330
  54.8 1.6 %reshape.16 = f32[64,4,128]{2,1,0:T(4,128)} reshape(f32[64,512]{1,0:T(8,128)} %get-tuple-element.4) | data formatting | bytes 262144 | tf_op jit(solution)/shard_map/reshape | solution.py:364
  56.4 1.8 %copy.12 = f32[12,64,128]{2,1,0:T(8,128)} copy(f32[12,64,128]{2,1,0:T(8,128)} %get-tuple-element.9) | data formatting | bytes 786432
  (1 shorter events, 0.0 us)

commit v4 on v3

--- a/solution.py
+++ b/solution.py
@@ -7,7 +7,7 @@
 from jax.sharding import PartitionSpec as P
 
 MESH = pl.DeviceIdType.MESH
-GROUP = 4
+GROUP = 16
 
 
 def extended(value, sides, width):
@@ -233,9 +233,10 @@
         xx, yy = at(uu, vv)
         return terms[inv[first(uu, vv, zs[t]) + k]] + r_a[t, xx, yy, k]
 
-    for t in range(nz):
-        a_[t].wait_recv()
-        for e in range(2):
+    for e in range(2):
+        for t in range(nz):
+            if e == 0:
+                a_[t].wait_recv()
             encode(s_b.at[t, e], [partial(t, 1 - u, v if e else 1 - v, k) for k in range(q)])
             b_[t, e].start()
 
@@ -249,15 +250,18 @@
         b_[t, 1].wait_recv()
         c_[t].wait_recv()
         came, more = decode(r_b.at[t, 1], q, nfac), decode(r_c.at[t], q, nfac)
-        for k in range(q):
-            s_d[t, k] = partial(t, u, v, k) + came[k] + more[k]
+        sums = [partial(t, u, v, k) + came[k] + more[k] for k in range(q)]
         if t < last:
+            encode(s_d.at[t], sums)
             d_[t].start()
-
-    stage_c(0)
-    for t in range(1, nz):
+        else:
+            for k in range(q):
+                s_e[k] = sums[k]
+
+    for t in range(nz):
         stage_c(t)
-        stage_d(t - 1)
+    for t in range(last):
+        stage_d(t)
 
     for h in halo:
         h.wait()
@@ -282,10 +286,11 @@
     for t in range(last):
         d_[t].wait_recv()
     near, over, pass_on = [], [], []
+    landed = [decode(r_d.at[t], q, nfac) for t in range(last)]
     for k in range(q):
-        total = s_d[last, k]
+        total = s_e[k]
         for t in range(last):
-            total = total + r_d[t, k]
+            total = total + landed[t][k]
         total = total / (spots * nx)
         s_e[k] = total
         over.append(remote(s_e.at[k], r_e.at[0, k], es.at[0, k], er.at[0, k], opp, j))
@@ -349,8 +354,8 @@
             pltpu.VMEM((nz, 2, q * nfac + 16, genes), jnp.int16),
             pltpu.VMEM((nz, q * nfac + 16, genes), jnp.int16),
             pltpu.VMEM((nz, q * nfac + 16, genes), jnp.int16),
-            pltpu.VMEM((nz, q, nfac, genes), f32),
-            pltpu.VMEM((nz - 1, q, nfac, genes), f32),
+            pltpu.VMEM((nz - 1, q * nfac + 16, genes), jnp.int16),
+            pltpu.VMEM((nz - 1, q * nfac + 16, genes), jnp.int16),
             pltpu.VMEM((q, nfac, genes), f32),
             pltpu.VMEM((3, q, nfac, genes), f32),
             dma, dma, dma((4,)), dma((4,)),
@@ -358,7 +363,7 @@
         + [dma((nz,))] * 2 + [dma((nz, 2))] * 2 + [dma((nz,))] * 2 + [dma((nz - 1,))] * 2
         + [dma((3, q))] * 2,
         compiler_params=pltpu.CompilerParams(
-            collective_id=0, has_side_effects=True, vmem_limit_bytes=60 * 1024 * 1024
+            collective_id=0, has_side_effects=True, vmem_limit_bytes=50 * 1024 * 1024
         ),
     )(ids, inv, live[0], loadings.reshape(nfac, spots), gene_factors, counts[0, 0])
     return grad_l.reshape(nfac, rows, cols), grad_g

time: 58.4 us -> 51.9 us (0.89)
  Pallas kernels: 50.7 us -> 45.7 us
  local copies, waits for them, and re-layouts: 4.85 us -> 3.87 us
  other arithmetic: 1.35 us -> 0.75 us
    pallas_call x1, Pallas kernels: 50.7 us -> 45.7 us  [by_kernel(): pl.pallas_call(functools.partial(kernel, nx, ny, rows), out_shape=(jax.Sh...]
    reshape x1, local copies, waits for them, and re-layouts: 1.6 us -> 0.7 us  [by_kernel(): return (grad_l.reshape(nfac, rows, cols), grad_g)]
    reduce_min x1, other arithmetic: 1.34 us -> 0.75 us  [by_kernel(): jnp.min(jnp.where(hit, slot[None, :], slots), axis=1).astype(jnp.int32)]
    unnamed x2 -> x6, local copies, waits for them, and re-layouts: 3.24 us -> 3.17 us
where the time goes in v4:
time: 51.9 us; the launch traced here: 51.7 us
  Pallas kernels  45.7 us (88%)
  local copies, waits for them, and re-layouts  3.87 us (7%)
  between operations  1.3 us (3%)
  other arithmetic  0.75 us (1%)
    pallas_call x1, Pallas kernels, by_kernel(): pl.pallas_call(functools.partial(kernel, nx, ny, rows), out_shape=(jax.Sh...  45.7 us
    unnamed x6, local copies, waits for them, and re-layouts  3.17 us

profile of v4, /device:TPU:0, one launch (start us, length us, event | category | flops | bytes accessed | tf_op | source)
XLA Modules:
  0.0 51.7 jit_solution(930055622904015096)
XLA Ops:
  1.3 0.7 %select_reduce_fusion.inv = s32[96]{0:T(128)S(1)} fusion(s32[32]{0:T(128)} %bitcast.11, pred[32]{0:T(512)(128)(4,1)S(1)} %iota_compare_fusion.1), kind=kLoop, calls=%fused_computation.1 | loop fusion | flops 12192 | bytes 544 | tf_op jit(solution)/shard_map/reduce_min | solution.py:330
  2.0 0.9 %copy.9 = bf16[8,8,4,128]{3,1,2,0:T(8,128)(2,1)S(1)} copy(bf16[8,8,4,128]{3,2,1,0:T(4,128)(2,1)} %bitcast.14) | data formatting | bytes 131072
  2.9 0.0 copy-start
  2.9 0.9 %copy-done = bf16[12,64,128]{2,1,0:T(8,128)(2,1)S(1)} copy-done((bf16[12,64,128]{2,1,0:T(8,128)(2,1)S(1)}, bf16[12,64,128]{2,1,0:T(8,128)(2,1)}, u32[]{:S(2)}) %copy-start) | copy-done | bytes 196632
  3.8 0.0 copy-start.1
  3.8 0.7 %copy-done.1 = s32[1,1,32]{2,1,0:T(1,128)S(1)} copy-done((s32[1,1,32]{2,1,0:T(1,128)S(1)}, s32[1,1,32]{2,1,0:T(1,128)}, u32[]{:S(2)}) %copy-start.1) | copy-done | bytes 152
  4.5 45.7 %shard_map.68 = (f32[64,512]{1,0:T(8,128)S(1)}, f32[12,64,128]{2,1,0:T(8,128)S(1)}) custom-call(s32[32]{0:T(128)S(1)} %bitcast.12, s32[96]{0:T(128)S(1)} %select_reduce_fusion.inv, s32[1]{0:T(128)} %bitcast.9.live, bf16[64,512]{1,0:T(8,128)(2,1)S(1)} %bitcast.10, bf16[12,64,128]{2,1,0:T(8,128)(2,1)S(1)} %copy-done, bf16[32,128,512]{2,1,0:T(8,128)(2,1)} %bitcast.13), custom_call_target="tpu_custom_call" | custom-call | tf_op jit(solution)/shard_map/pallas_call | solution.py:335
  50.2 0.7 %reshape.16 = f32[64,4,128]{2,1,0:T(4,128)} reshape(f32[64,512]{1,0:T(8,128)S(1)} %get-tuple-element.4) | data formatting | bytes 262144 | tf_op jit(solution)/shard_map/reshape | solution.py:369
  50.9 0.7 %copy.12 = f32[12,64,128]{2,1,0:T(8,128)} copy(f32[12,64,128]{2,1,0:T(8,128)S(1)} %get-tuple-element.9) | data formatting | bytes 786432
  (1 shorter events, 0.0 us)
Async XLA Ops:
  2.9 0.9 %copy-start = (bf16[12,64,128]{2,1,0:T(8,128)(2,1)S(1)}, bf16[12,64,128]{2,1,0:T(8,128)(2,1)}, u32[]{:S(2)}) copy-start(bf16[12,64,128]{2,1,0:T(8,128)(2,1)} %gf.1) | copy-start | bytes 589828
  3.8 0.7 %copy-start.1 = (s32[1,1,32]{2,1,0:T(1,128)S(1)}, s32[1,1,32]{2,1,0:T(1,128)}, u32[]{:S(2)}) copy-start(s32[1,1,32]{2,1,0:T(1,128)} %param.8) | copy-start | bytes 388
